TPU v7x, 512 devices: a whole 4x4x16 slice. The times are simulated.
512 devices in a mesh: expert: 128 (over z, x, core), rep: 4 (over y).
Axes of the slice: x: 4, y: 4, z: 16, core: 2. Of those that a mesh axis runs over, the one named last changes fastest.
Arguments:
- tokens: bfloat16 [512, 256, 1280], P(('rep', 'expert')), parts along dimension 0, may hold values from -48 to 48, as said below
- slot_weight: bfloat16 [5120, 16], P('rep'), parts along dimension 0, may hold values from -1 to 1, as said below
- w_in: bfloat16 [1280, 81920], P(None, 'expert'), may hold values from -0.15625 to 0.15625
- w_out: bfloat16 [81920, 1280], P('expert'), may hold values from -0.078125 to 0.078125
Outputs:
- mixed: bfloat16 [512, 256, 1280], P(('rep', 'expert')), parts along dimension 0
There are 4 independent parts, one for each index of `rep`. A program takes and returns all parts, laid end to end along the dimension named above; an argument that names none is the same for every part. Nothing has to cross between parts.
Inputs may be any that keep to these rules, and one draw needn't show every extreme that they name: `tokens`: activations mostly of order one. `slot_weight`: entries of deviation 1280 ** -0.5.
All inputs are finite; a program needn't handle non-finite values.
Results may differ from a plain program's by a relative error of at most 0.015.
Values may be sent and summed in bfloat16 or wider, within the bound.
A program may use at most 64 MiB of HBM per device.

v0:
```python
import jax
import jax.numpy as jnp
from jax import lax
from jax.sharding import PartitionSpec as P


def on_device(tokens, slot_weight, w_in, w_out):
    devices = lax.axis_size("expert")
    experts = slot_weight.shape[1]
    split = devices // experts
    images = tokens.shape[0]
    width = tokens.shape[2]
    logits = jnp.einsum("btd,de->bte", tokens, slot_weight, preferred_element_type=jnp.float32)
    dispatch = jax.nn.softmax(logits, axis=1).astype(jnp.bfloat16)
    slots = jnp.einsum("bte,btd->bed", dispatch, tokens, preferred_element_type=jnp.float32).astype(
        jnp.bfloat16
    )
    copies = jnp.repeat(slots, split, axis=1)
    arrived = lax.all_to_all(copies, "expert", split_axis=1, concat_axis=0, tiled=True)
    mine = arrived.reshape(arrived.shape[0], width)
    hidden = jax.nn.gelu(jnp.dot(mine, w_in, preferred_element_type=jnp.float32)).astype(
        jnp.bfloat16
    )
    partial_out = jnp.dot(hidden, w_out, preferred_element_type=jnp.float32).astype(jnp.bfloat16)
    returned = lax.all_to_all(
        partial_out.reshape(devices, images, width),
        "expert",
        split_axis=0,
        concat_axis=0,
        tiled=True,
    )
    expert_out = jnp.sum(
        returned.reshape(experts, split, images, width).astype(jnp.float32), axis=1
    ).astype(jnp.bfloat16)
    combine = jax.nn.softmax(logits, axis=2).astype(jnp.bfloat16)
    mixed = jnp.einsum("bte,ebd->btd", combine, expert_out, preferred_element_type=jnp.float32)
    return mixed.astype(jnp.bfloat16)


def solution(mesh):
    in_specs = (
        P(("rep", "expert"), None, None),
        P("rep", None),
        P(None, "expert"),
        P("expert", None),
    )
    out_specs = P(("rep", "expert"), None, None)
    return jax.shard_map(
        on_device, mesh=mesh, in_specs=in_specs, out_specs=out_specs, check_vma=False
    )
```

profile of v0, /device:TPU:1, one launch (start us, length us, event | category | flops | bytes accessed | tf_op | source)
XLA Modules:
  0.0 86.9 jit_solution(5112106949295419672)
XLA Ops:
  0.0 0.0 copy-start
  0.0 1.6 %fusion.35 = (f32[256]{0:T(256)S(1)}, f32[16]{0:T(128)S(1)}, f32[256,16]{0,1:T(8,128)S(1)}) fusion(bf16[1280,16]{0,1:T(8,128)(2,1)} %param.5, bf16[1,256,1280]{2,1,0:T(8,128)(2,1)} %param.4), kind=kOutput, calls=%fused_computation.40 | convolution fusion | flops 10493680 | bytes 713792 | tf_op jit(solution)/shard_map/btd,de->bte/dot_general | solution.py:13
  1.6 0.2 fusion.25
  1.8 1.3 %convolution_convert_fusion.2 = bf16[16,1280]{1,0:T(8,128)(2,1)S(1)} fusion(bf16[1,256,1280]{2,1,0:T(8,128)(2,1)} %param.4, f32[256,16]{0,1:T(8,128)S(1)} %get-tuple-element.9, f32[16]{0:T(128)S(1)} %get-tuple-element.6, f32[16]{0:T(128)S(1)} %get-tuple-element.8), kind=kOutput, calls=%fused_computation.4 | convolution fusion | flops 10518528 | bytes 712832 | tf_op jit(solution)/shard_map/bte,btd->bed/dot_general | solution.py:15
  3.2 0.1 broadcast_bitcast_fusion
  3.2 0.5 copy.17
  3.8 0.5 broadcast.17
  4.3 2.7 %reduce.10 = bf16[128,1280]{1,0:T(8,128)(2,1)S(1)} reduce(bf16[128,1,1280]{2,1,0:T(2,128)(2,1)S(1)} %bitcast.30, bf16[]{:T(256)} %broadcast.17), dimensions={1}, to_apply=%bitcast.29.reduce_sub_computation | reduce | bytes 655362
  7.0 0.1 reshape.67
  7.0 43.2 %all_to_all.14 = bf16[128,2,640]{2,1,0:T(2,128)(2,1)S(1)} all-to-all(bf16[128,2,640]{2,1,0:T(2,128)(2,1)S(1)} %reshape.67), channel_id=1, replica_groups=mesh['expert'=128,'rep'=4] {'expert'}, dimensions={0} | all-to-all | bytes 655360 | tf_op jit(solution)/shard_map/all_to_all | solution.py:19
  50.2 0.3 reshape.68
  50.5 0.0 copy-done
  50.5 2.3 %fusion.1 = bf16[128,1,1280]{2,0,1:T(8,128)(2,1)S(1)} fusion(bf16[640,1280]{1,0:T(8,128)(2,1)S(1)} %copy-done, bf16[1280,640]{1,0:T(8,128)(2,1)} %param.6, bf16[1,128,1280]{2,0,1:T(2,128)(2,1)S(1)} %bitcast.31), kind=kOutput, calls=%fused_computation.3 | convolution fusion | flops 420331520 | bytes 3932160 | tf_op jit(solution)/shard_map/dot_general | solution.py:24
  52.8 0.8 reduce.11
  53.7 0.1 reshape.69
  53.8 31.4 %all_to_all.15 = bf16[128,2,640]{2,1,0:T(2,128)(2,1)S(1)} all-to-all(bf16[128,2,640]{2,1,0:T(2,128)(2,1)S(1)} %reshape.69), channel_id=1, replica_groups=mesh['expert'=128,'rep'=4] {'expert'}, dimensions={0} | all-to-all | bytes 655360 | tf_op jit(solution)/shard_map/all_to_all | solution.py:25
  85.1 0.3 reshape.70
  85.4 0.2 bitcast_reduce_fusion
  85.7 1.2 %fusion = bf16[1,256,1280]{2,1,0:T(8,128)(2,1)} fusion(bf16[16,1280]{1,0:T(8,128)(2,1)S(1)} %bitcast_reduce_fusion, f32[256,16]{0,1:T(8,128)S(1)} %get-tuple-element.9, f32[256]{0:T(256)S(1)} %get-tuple-element.5, f32[256]{0:T(256)S(1)} %get-tuple-element.7), kind=kOutput, calls=%fused_computation.1 | convolution fusion | flops 10825728 | bytes 714752 | tf_op jit(solution)/shard_map/bte,ebd->btd/dot_general | solution.py:36
Async XLA Ops:
  0.0 50.5 %copy-start = (bf16[640,1280]{1,0:T(8,128)(2,1)S(1)}, bf16[640,1280]{1,0:T(8,128)(2,1)}, u32[]{:S(2)}) copy-start(bf16[640,1280]{1,0:T(8,128)(2,1)} %param.7) | copy-start | bytes 4915204
where the time goes:
time: 88.5 us; the launch traced here: 86.9 us
  blocking collectives  74.6 us (84%)
  matrix products  6.48 us (7%)
  other arithmetic  3.96 us (4%)
  local copies, waits for them, and re-layouts  1.77 us (2%)
    all_to_all x1, blocking collectives, on_device(): lax.all_to_all(copies, 'expert', split_axis=1, concat_axis=0, tiled=True)  43.2 us
    all_to_all x1, blocking collectives, on_device(): lax.all_to_all(partial_out.reshape(devices, images, width), 'expert', spl...  31.4 us
    unnamed x1, other arithmetic  2.68 us
    dot_general x1, matrix products, on_device(): jnp.dot(hidden, w_out, preferred_element_type=jnp.float32)  2.29 us

commit v1 on v0

v1 whole, which is shorter than its diff:
```python
import functools

import jax
import jax.numpy as jnp
from jax import lax
from jax.experimental import pallas as pl
from jax.experimental.pallas import tpu as pltpu
from jax.sharding import PartitionSpec as P

BF16 = jnp.bfloat16
F32 = jnp.float32
CORES = 2


def remote(src, dst, send_sem, recv_sem, target):
    return pltpu.make_async_remote_copy(
        src_ref=src,
        dst_ref=dst,
        send_sem=send_sem,
        recv_sem=recv_sem,
        device_id={"expert": target},
        device_id_type=pl.DeviceIdType.MESH,
    )


def kernel(
    planes,
    columns,
    tokens_hbm,
    slot_ref,
    w_in_hbm,
    w_out_hbm,
    out_ref,
    tokens,
    w_in,
    w_out,
    slot_out,
    slot_in,
    gathered,
    to_core,
    from_core,
    to_column,
    from_column,
    expert_out,
    expert_in,
    load_sem,
    z_send,
    z_recv,
    x_send,
    x_recv,
    c_send,
    c_recv,
):
    side = columns * CORES
    half = columns * planes
    me = lax.axis_index("expert")
    core = lax.rem(me, CORES)
    column = lax.rem(lax.div(me, CORES), columns)
    plane = lax.div(me, side)
    mate = me + 1 - 2 * core

    def in_plane(step):
        return lax.rem(plane + step, planes)

    def at_plane(other):
        return me + (other - plane) * side

    def in_column(step):
        return lax.rem(column + step, columns)

    def at_column(other):
        return me + (other - column) * CORES

    load_tokens = pltpu.make_async_copy(tokens_hbm, tokens, load_sem.at[0])
    load_in = pltpu.make_async_copy(w_in_hbm, w_in, load_sem.at[1])
    load_out = pltpu.make_async_copy(w_out_hbm, w_out, load_sem.at[2])
    load_tokens.start()
    load_in.start()
    load_out.start()
    barrier = pltpu.get_barrier_semaphore()
    peers = [at_plane(in_plane(k)) for k in range(1, planes)]
    peers += [at_column(in_column(k)) for k in range(1, columns)]
    peers += [mate]
    for peer in peers:
        pl.semaphore_signal(
            barrier, inc=1, device_id={"expert": peer}, device_id_type=pl.DeviceIdType.MESH
        )

    load_tokens.wait()
    logits = lax.dot_general(
        slot_ref[...], tokens[0], (((1,), (1,)), ((), ())), preferred_element_type=F32
    )
    top = jnp.max(logits, axis=1, keepdims=True)
    weight = jnp.exp(logits - top)
    dispatch = (weight / jnp.sum(weight, axis=1, keepdims=True)).astype(BF16)
    slots = jnp.dot(dispatch, tokens[0], preferred_element_type=F32)
    slot_out[...] = slots.reshape(slot_out.shape).astype(BF16)

    pl.semaphore_wait(barrier, len(peers))
    order = sorted(range(1, planes), key=lambda k: -min(k, planes - k))
    for k in order:
        to = in_plane(k)
        remote(slot_out.at[to], slot_in.at[plane], z_send.at[0], z_recv.at[0], at_plane(to)).start()
    slot_in[plane] = slot_out[plane]
    top = jnp.max(logits, axis=0, keepdims=True)
    weight = jnp.exp(logits - top)
    combine = (weight / jnp.sum(weight, axis=0, keepdims=True)).astype(BF16)
    arrived = slot_in.at[pl.ds(0, planes - 1)]
    pltpu.make_async_copy(arrived, arrived, z_recv.at[0]).wait()

    def block(c, x):
        return pl.ds(pl.multiple_of((c * columns + x) * planes, planes), planes)

    mine = block(core, column)
    gathered[mine, :] = slot_in[...].reshape(planes, -1)
    first = [
        remote(gathered.at[mine], gathered.at[mine], x_send.at[k], x_recv.at[k], at_column(in_column(k)))
        for k in range(1, columns)
    ]
    for copy in first:
        copy.start()
    relays = [remote(gathered.at[mine], gathered.at[mine], c_send.at[0], c_recv.at[0], mate)]
    relays[0].start()
    for k in range(1, columns):
        came = block(core, in_column(columns - k))
        here = gathered.at[came]
        pltpu.make_async_copy(here, here, x_recv.at[k]).wait()
        relays.append(remote(here, here, c_send.at[k], c_recv.at[k], mate))
        relays[-1].start()
    for relay in relays:
        relay.wait_recv()

    load_in.wait()
    hidden = jnp.dot(gathered[...], w_in[...], preferred_element_type=F32)
    hidden = jax.nn.gelu(hidden).astype(BF16)
    load_out.wait()
    partial_out = jnp.dot(hidden, w_out[...], preferred_element_type=F32)
    is_zero = core == 0
    upper, lower = partial_out[:half], partial_out[half:]
    to_core[...] = jnp.where(is_zero, lower, upper).astype(BF16)
    swap = remote(to_core, from_core, c_send.at[columns], c_recv.at[columns], mate)
    swap.start()
    kept = jnp.where(is_zero, upper, lower)
    swap.wait_recv()
    both = kept + from_core[...].astype(F32)
    to_column[...] = both.reshape(columns, planes, -1).astype(BF16)
    second = []
    for k in range(1, columns):
        to = in_column(k)
        second.append(
            remote(to_column.at[to], from_column.at[k], x_send.at[columns + k], x_recv.at[columns + k], at_column(to))
        )
        second[-1].start()
    total = to_column[column].astype(F32)
    for k in range(1, columns):
        second[k - 1].wait_recv()
        total = total + from_column[k].astype(F32)

    expert_out[...] = total.reshape(expert_out.shape).astype(BF16)
    for k in order:
        to = in_plane(k)
        remote(expert_out.at[to], expert_in.at[plane], z_send.at[1], z_recv.at[1], at_plane(to)).start()
    expert_in[plane] = expert_out[plane]
    arrived = expert_in.at[pl.ds(0, planes - 1)]
    pltpu.make_async_copy(arrived, arrived, z_recv.at[1]).wait()
    mixed = lax.dot_general(
        combine,
        expert_in[...].reshape(planes, -1),
        (((0,), (0,)), ((), ())),
        preferred_element_type=F32,
    )
    out_ref[0] = mixed.astype(BF16)

    for buffer, number in ((slot_out, 0), (expert_out, 1)):
        left = buffer.at[pl.ds(0, planes - 1)]
        pltpu.make_async_copy(left, left, z_send.at[number]).wait()
    for copy in first + relays + [swap] + second:
        copy.wait_send()


def on_device(tokens, slot_weight, w_in, w_out, *, devices, cores_per_chip):
    images, patches, width = tokens.shape
    experts = slot_weight.shape[1]
    units = w_in.shape[1]
    planes = experts
    columns = devices // planes // cores_per_chip
    half = columns * planes
    dma = pltpu.SemaphoreType.DMA
    return pl.pallas_call(
        functools.partial(kernel, planes, columns),
        out_shape=jax.ShapeDtypeStruct(tokens.shape, BF16),
        in_specs=[
            pl.BlockSpec(memory_space=pltpu.HBM),
            pl.BlockSpec(memory_space=pltpu.VMEM),
            pl.BlockSpec(memory_space=pltpu.HBM),
            pl.BlockSpec(memory_space=pltpu.HBM),
        ],
        out_specs=pl.BlockSpec(memory_space=pltpu.VMEM),
        scratch_shapes=[
            pltpu.VMEM(tokens.shape, BF16),
            pltpu.VMEM((width, units), BF16),
            pltpu.VMEM((units, width), BF16),
            pltpu.VMEM((planes, 2, width // 2), BF16),
            pltpu.VMEM((planes, 2, width // 2), BF16),
            pltpu.VMEM((2 * half, width), BF16),
            pltpu.VMEM((half, width), BF16),
            pltpu.VMEM((half, width), BF16),
            pltpu.VMEM((columns, planes, width), BF16),
            pltpu.VMEM((columns, planes, width), BF16),
            pltpu.VMEM((planes, 2, width // 2), BF16),
            pltpu.VMEM((planes, 2, width // 2), BF16),
            dma((3,)),
            dma((2,)),
            dma((2,)),
            dma((2 * columns,)),
            dma((2 * columns,)),
            dma((columns + 1,)),
            dma((columns + 1,)),
        ],
        compiler_params=pltpu.CompilerParams(
            collective_id=0, has_side_effects=True, vmem_limit_bytes=56 * 1024 * 1024
        ),
        cost_estimate=pl.CostEstimate(
            flops=2 * 2 * devices * width * units, bytes_accessed=4 * width * units, transcendentals=0
        ),
    )(tokens, slot_weight.T, w_in, w_out)


def solution(mesh):
    in_specs = (
        P(("rep", "expert"), None, None),
        P("rep", None),
        P(None, "expert"),
        P("expert", None),
    )
    out_specs = P(("rep", "expert"), None, None)
    step = functools.partial(on_device, devices=mesh.shape["expert"], cores_per_chip=CORES)
    return jax.shard_map(step, mesh=mesh, in_specs=in_specs, out_specs=out_specs, check_vma=False)
```

time: 88.5 us -> 45.3 us (0.51)
  the two profiles are of different devices: /device:TPU:1 before, /device:TPU:24 now
where the time goes in v1:
time: 45.3 us; the launch traced here: 45.1 us
  Pallas kernels  43.1 us (95%)
  local copies, waits for them, and re-layouts  1.97 us (4%)
    pallas_call x1, Pallas kernels, on_device(): pl.pallas_call(functools.partial(kernel, planes, columns), out_shape=jax....  43.1 us
    unnamed x1, local copies, waits for them, and re-layouts  1.97 us

profile of v1, /device:TPU:24, one launch (start us, length us, event | category | flops | bytes accessed | tf_op | source)
XLA Modules:
  0.0 45.1 jit_solution(3906975078219424316)
XLA Ops:
  0.0 43.1 %shard_map.46 = bf16[1,256,1280]{2,1,0:T(8,128)(2,1)} custom-call(bf16[1,256,1280]{2,1,0:T(8,128)(2,1)} %tokens_hbm.1, bf16[16,1280]{1,0:T(8,128)(2,1)} %bitcast.1, bf16[1280,640]{1,0:T(8,128)(2,1)} %w_in_hbm.1, bf16[640,1280]{1,0:T(8,128)(2,1)} %w_out_hbm.1), custom_call_target="tpu_custom_call" | custom-call | flops 419430400 | bytes 3276800 | tf_op jit(solution)/shard_map/pallas_call | solution.py:189
  43.1 2.0 %copy.6 = bf16[1,256,1280]{2,1,0:T(8,128)(2,1)} copy(bf16[1,256,1280]{2,1,0:T(8,128)(2,1)} %shard_map.46) | data formatting | bytes 1310720

commit v2 on v0

v2 whole, which is shorter than its diff:
```python
import functools

import jax
import jax.numpy as jnp
from jax import lax
from jax.experimental import pallas as pl
from jax.experimental.pallas import tpu as pltpu
from jax.sharding import PartitionSpec as P

BF16 = jnp.bfloat16
F32 = jnp.float32
CORES = 2
CUTS = (0, 4, 8)


def remote(src, dst, send_sem, recv_sem, target):
    return pltpu.make_async_remote_copy(
        src_ref=src,
        dst_ref=dst,
        send_sem=send_sem,
        recv_sem=recv_sem,
        device_id={"expert": target},
        device_id_type=pl.DeviceIdType.MESH,
    )


def wait_for(rows, sem):
    pltpu.make_async_copy(rows, rows, sem).wait()


def kernel(
    planes,
    side,
    tokens_hbm,
    slot_ref,
    w_in_hbm,
    w_out_hbm,
    combine_ref,
    expert_ref,
    tokens,
    w_in,
    w_out,
    slot_out,
    slots,
    partial,
    scattered,
    expert_out,
    expert_in,
    load_sem,
    send_sem,
    recv_sem,
):
    chunks = list(zip(CUTS, CUTS[1:] + (planes,)))
    count = len(chunks)
    slots, partial, scattered = (
        [ref.at[pl.ds(side * low, side * (high - low))] for low, high in chunks]
        for ref in (slots, partial, scattered)
    )
    me = lax.axis_index("expert")
    place = lax.rem(me, side)
    plane = lax.div(me, side)

    def in_plane(step):
        return lax.rem(plane + step, planes)

    def at_plane(other):
        return other * side + place

    def in_side(step):
        return lax.rem(place + step, side)

    def at_place(other):
        return plane * side + other

    load_tokens = pltpu.make_async_copy(tokens_hbm, tokens, load_sem.at[0])
    load_in = pltpu.make_async_copy(w_in_hbm, w_in, load_sem.at[1])
    load_out = pltpu.make_async_copy(w_out_hbm, w_out, load_sem.at[2])
    load_tokens.start()
    barrier = pltpu.get_barrier_semaphore()
    far_first = sorted(range(1, planes), key=lambda k: -min(k, planes - k))
    peers = [at_plane(in_plane(k)) for k in far_first]
    peers += [at_place(in_side(k)) for k in range(1, side)]
    for peer in peers:
        pl.semaphore_signal(
            barrier, inc=1, device_id={"expert": peer}, device_id_type=pl.DeviceIdType.MESH
        )
    load_in.start()
    load_out.start()

    load_tokens.wait()
    logits = lax.dot_general(
        slot_ref[...], tokens[0], (((1,), (1,)), ((), ())), preferred_element_type=F32
    )
    top = jnp.max(logits, axis=1, keepdims=True)
    weight = jnp.exp(logits - top)
    dispatch = (weight / jnp.sum(weight, axis=1, keepdims=True)).astype(BF16)
    own_slots = jnp.dot(dispatch, tokens[0], preferred_element_type=F32)
    slot_out[...] = own_slots.reshape(slot_out.shape).astype(BF16)

    pl.semaphore_wait(barrier, len(peers))

    def send_slots(landing, sem):
        for k in far_first:
            to = in_plane(k)
            remote(slot_out.at[to], landing, send_sem.at[0], sem, at_plane(to)).start()
        pltpu.make_async_copy(slot_out.at[plane], landing, sem).start()

    for number, (low, high) in enumerate(chunks):

        @pl.when(jnp.logical_and(plane >= low, plane < high))
        def _():
            send_slots(slots[number].at[place * (high - low) + plane - low], recv_sem.at[number])

    top = jnp.max(logits, axis=0, keepdims=True)
    weight = jnp.exp(logits - top)
    combine_ref[...] = (weight / jnp.sum(weight, axis=0, keepdims=True)).astype(BF16)

    def spread(number):
        low, high = chunks[number]
        block = slots[number].at[pl.ds(place * (high - low), high - low)]
        wait_for(block, recv_sem.at[number])
        for k in range(1, side):
            remote(
                block, block, send_sem.at[1 + number], recv_sem.at[count + number], at_place(in_side(k))
            ).start()

    def experts(number):
        low, high = chunks[number]
        rows = high - low
        wait_for(slots[number].at[pl.ds(0, (side - 1) * rows)], recv_sem.at[count + number])
        hidden = jnp.dot(
            slots[number][...].reshape(side * rows, -1), w_in[...], preferred_element_type=F32
        )
        hidden = jax.nn.gelu(hidden).astype(BF16)
        out = jnp.dot(hidden, w_out[...], preferred_element_type=F32)
        partial[number][...] = out.reshape(partial[number].shape).astype(BF16)
        block = scattered[number].at[pl.ds(place * rows, rows)]
        sem = recv_sem.at[2 * count + number]
        for k in range(1, side):
            to = in_side(k)
            remote(
                partial[number].at[pl.ds(to * rows, rows)], block, send_sem.at[1 + count + number], sem, at_place(to)
            ).start()
        pltpu.make_async_copy(partial[number].at[pl.ds(place * rows, rows)], block, sem).start()

    def finish(number):
        low, high = chunks[number]
        rows = high - low
        wait_for(scattered[number], recv_sem.at[2 * count + number])
        total = jnp.zeros((rows * 2, scattered[number].shape[2]), F32)
        for k in range(side):
            part = scattered[number][k * rows : (k + 1) * rows]
            total = total + part.reshape(total.shape).astype(F32)
        expert_out[low:high] = total.astype(BF16).reshape(rows, 2, -1)
        for target in range(low, high):
            own = expert_out.at[target]

            @pl.when(plane == target)
            def _():
                pltpu.make_async_copy(own, expert_in.at[plane], recv_sem.at[3 * count]).start()

            @pl.when(plane != target)
            def _():
                remote(
                    own, expert_in.at[plane], send_sem.at[1 + 2 * count], recv_sem.at[3 * count], at_plane(target)
                ).start()

    spread(0)
    spread(1)
    load_in.wait()
    load_out.wait()
    experts(0)
    spread(2)
    experts(1)
    finish(0)
    experts(2)
    finish(1)
    finish(2)

    wait_for(expert_in, recv_sem.at[3 * count])
    expert_ref[...] = expert_in[...].reshape(expert_ref.shape)

    wait_for(slot_out.at[pl.ds(0, planes - 1)], send_sem.at[0])
    for number, (low, high) in enumerate(chunks):
        others = pl.ds(0, (side - 1) * (high - low))
        wait_for(slots[number].at[others], send_sem.at[1 + number])
        wait_for(partial[number].at[others], send_sem.at[1 + count + number])
    wait_for(expert_out.at[pl.ds(0, planes - 1)], send_sem.at[1 + 2 * count])


def on_device(tokens, slot_weight, w_in, w_out, *, devices):
    images, patches, width = tokens.shape
    experts = slot_weight.shape[1]
    units = w_in.shape[1]
    planes = experts
    side = devices // planes
    dma = pltpu.SemaphoreType.DMA

    def rows(count):
        return pltpu.VMEM((count, 2, width // 2), BF16)

    vmem = pl.BlockSpec(memory_space=pltpu.VMEM)
    hbm = pl.BlockSpec(memory_space=pltpu.HBM)
    combine, expert_out = pl.pallas_call(
        functools.partial(kernel, planes, side),
        out_shape=[
            pltpu.VMEM((experts, patches), BF16),
            pltpu.VMEM((experts, width), BF16),
        ],
        in_specs=[hbm, vmem, hbm, hbm],
        out_specs=[vmem, vmem],
        scratch_shapes=[
            pltpu.VMEM(tokens.shape, BF16),
            pltpu.VMEM((width, units), BF16),
            pltpu.VMEM((units, width), BF16),
            rows(planes),
            rows(devices),
            rows(devices),
            rows(devices),
            rows(planes),
            rows(planes),
            dma((3,)),
            dma((2 + 2 * len(CUTS),)),
            dma((1 + 3 * len(CUTS),)),
        ],
        compiler_params=pltpu.CompilerParams(
            collective_id=0, has_side_effects=True, vmem_limit_bytes=60 * 1024 * 1024
        ),
        cost_estimate=pl.CostEstimate(
            flops=2 * 2 * devices * width * units, bytes_accessed=4 * width * units, transcendentals=0
        ),
    )(tokens, slot_weight.T, w_in, w_out)
    mixed = lax.dot_general(
        combine, expert_out, (((0,), (0,)), ((), ())), preferred_element_type=F32
    )
    return mixed.astype(BF16).reshape(tokens.shape)


def solution(mesh):
    in_specs = (
        P(("rep", "expert"), None, None),
        P("rep", None),
        P(None, "expert"),
        P("expert", None),
    )
    out_specs = P(("rep", "expert"), None, None)
    step = functools.partial(on_device, devices=mesh.shape["expert"])
    return jax.shard_map(step, mesh=mesh, in_specs=in_specs, out_specs=out_specs, check_vma=False)
```

time: 88.5 us -> 40.6 us (0.46); the launches traced: 86.9 us -> 40.4 us
  blocking collectives: 74.6 us -> 0 us
  Pallas kernels: 0 us -> 39.2 us
  matrix products: 6.48 us -> 1.2 us
  other arithmetic: 3.96 us -> 0 us
  local copies, waits for them, and re-layouts: 1.77 us -> 0 us
    all_to_all x2 -> x0, blocking collectives: 74.6 us -> none  [the longest x1 43.2 us: on_device(): lax.all_to_all(copies, 'expert', split_axis=1, concat_axis=0, tiled=True)]
    pallas_call x0 -> x1, Pallas kernels: none -> 39.2 us  [on_device(): pl.pallas_call(functools.partial(kernel, planes, side), out_shape=[pltpu....]
    dot_general x4 -> x1, matrix products: 6.48 us -> 1.2 us  [on_device(): lax.dot_general(combine, expert_out, (((0,), (0,)), ((), ())), preferred_...]
    unnamed x1 -> x0, other arithmetic: 2.68 us -> none
    unnamed x7 -> x0, local copies, waits for them, and re-layouts: 1.21 us -> none
where the time goes in v2:
time: 40.6 us; the launch traced here: 40.4 us
  Pallas kernels  39.2 us (97%)
  matrix products  1.2 us (3%)
    pallas_call x1, Pallas kernels, on_device(): pl.pallas_call(functools.partial(kernel, planes, side), out_shape=[pltpu....  39.2 us
    dot_general x1, matrix products, on_device(): lax.dot_general(combine, expert_out, (((0,), (0,)), ((), ())), preferred_...  1.2 us

profile of v2, /device:TPU:1, one launch (start us, length us, event | category | flops | bytes accessed | tf_op | source)
XLA Modules:
  0.0 40.4 jit_solution(8855029046636610827)
XLA Ops:
  0.0 39.2 %shard_map.46 = (bf16[16,256]{1,0:T(8,128)(2,1)S(1)}, bf16[16,1280]{1,0:T(8,128)(2,1)S(1)}) custom-call(bf16[1,256,1280]{2,1,0:T(8,128)(2,1)} %tokens_hbm.1, bf16[16,1280]{1,0:T(8,128)(2,1)} %bitcast.5, bf16[1280,640]{1,0:T(8,128)(2,1)} %w_in_hbm.1, bf16[640,1280]{1,0:T(8,128)(2,1)} %w_out_hbm.1), custom_call_target="tpu_custom_call" | custom-call | flops 419430400 | bytes 3276800 | tf_op jit(solution)/shard_map/pallas_call | solution.py:204
  39.2 1.2 %fusion = bf16[1,256,1280]{2,1,0:T(8,128)(2,1)} fusion(bf16[16,256]{1,0:T(8,128)(2,1)S(1)} %get-tuple-element.7, bf16[16,1280]{1,0:T(8,128)(2,1)S(1)} %get-tuple-element.8), kind=kOutput, calls=%fused_computation.1 | convolution fusion | flops 10813440 | bytes 704512 | tf_op jit(solution)/shard_map/dot_general | solution.py:233

commit v3 on v2

--- a/solution.py
+++ b/solution.py
@@ -11,6 +11,11 @@
 F32 = jnp.float32
 CORES = 2
 CUTS = (0, 4, 8)
+EARLY = CUTS[1]
+LOWER = CUTS[2]
+HOP = 4
+VIA = (7, 8, 9)
+LAST = LOWER + HOP
 
 
 def remote(src, dst, send_sem, recv_sem, target):
@@ -41,6 +46,8 @@
     w_in,
     w_out,
     slot_out,
+    relay,
+    relay_back,
     slots,
     partial,
     scattered,
@@ -49,6 +56,9 @@
     load_sem,
     send_sem,
     recv_sem,
+    ready_sem,
+    go_sem,
+    relay_sem,
 ):
     chunks = list(zip(CUTS, CUTS[1:] + (planes,)))
     count = len(chunks)
@@ -60,8 +70,10 @@
     place = lax.rem(me, side)
     plane = lax.div(me, side)
 
-    def in_plane(step):
-        return lax.rem(plane + step, planes)
+    is_early = plane < EARLY
+    is_high = plane >= LOWER
+    is_middle = jnp.logical_and(plane >= EARLY, plane < LOWER)
+    is_last = plane >= LAST
 
     def at_plane(other):
         return other * side + place
@@ -71,19 +83,52 @@
 
     def at_place(other):
         return plane * side + other
+
+    def tell(sem, target):
+        pl.semaphore_signal(
+            sem, inc=1, device_id={"expert": target}, device_id_type=pl.DeviceIdType.MESH
+        )
 
     load_tokens = pltpu.make_async_copy(tokens_hbm, tokens, load_sem.at[0])
     load_in = pltpu.make_async_copy(w_in_hbm, w_in, load_sem.at[1])
     load_out = pltpu.make_async_copy(w_out_hbm, w_out, load_sem.at[2])
     load_tokens.start()
     barrier = pltpu.get_barrier_semaphore()
-    far_first = sorted(range(1, planes), key=lambda k: -min(k, planes - k))
-    peers = [at_plane(in_plane(k)) for k in far_first]
-    peers += [at_place(in_side(k)) for k in range(1, side)]
-    for peer in peers:
-        pl.semaphore_signal(
-            barrier, inc=1, device_id={"expert": peer}, device_id_type=pl.DeviceIdType.MESH
-        )
+
+    @pl.when(is_last)
+    def _():
+        pl.semaphore_wait(barrier, EARLY)
+
+    @pl.when(jnp.logical_and(is_high, jnp.logical_not(is_last)))
+    def _():
+        pl.semaphore_wait(barrier, LOWER)
+
+    @pl.when(jnp.logical_not(is_high))
+    def _():
+        for other in range(1, LAST):
+
+            @pl.when(plane < other)
+            def _():
+                tell(barrier, at_plane(other))
+
+        @pl.when(is_early)
+        def _():
+            for other in range(LAST, planes):
+                tell(barrier, at_plane(other))
+
+        for k in range(1, side):
+            tell(barrier, at_place(in_side(k)))
+        pl.semaphore_wait(barrier, plane + (side - 1))
+
+    for other in range(LOWER):
+        answers = plane > other
+        if other >= EARLY:
+            answers = jnp.logical_and(answers, jnp.logical_not(is_last))
+
+        @pl.when(answers)
+        def _():
+            tell(ready_sem.at[plane], at_plane(other))
+
     load_in.start()
     load_out.start()
 
@@ -97,19 +142,139 @@
     own_slots = jnp.dot(dispatch, tokens[0], preferred_element_type=F32)
     slot_out[...] = own_slots.reshape(slot_out.shape).astype(BF16)
 
-    pl.semaphore_wait(barrier, len(peers))
-
-    def send_slots(landing, sem):
-        for k in far_first:
-            to = in_plane(k)
-            remote(slot_out.at[to], landing, send_sem.at[0], sem, at_plane(to)).start()
+    def send_to(e, landing, sem):
+        remote(slot_out.at[e], landing, send_sem.at[0], sem, at_plane(e)).start()
+
+    def keep(landing, sem):
         pltpu.make_async_copy(slot_out.at[plane], landing, sem).start()
 
-    for number, (low, high) in enumerate(chunks):
-
-        @pl.when(jnp.logical_and(plane >= low, plane < high))
+    @pl.when(is_early)
+    def _():
+        landing, sem = slots[0].at[place * EARLY + plane], recv_sem.at[0]
+        keep(landing, sem)
+
+        def send(e):
+            by_way = jnp.logical_and(e >= plane + VIA[0], e <= plane + VIA[-1])
+            by_way = jnp.logical_and(by_way, e < LAST)
+
+            @pl.when(plane > e)
+            def _():
+                send_to(e, landing, sem)
+
+            @pl.when(jnp.logical_and(plane < e, jnp.logical_not(by_way)))
+            def _():
+                pl.semaphore_wait(ready_sem.at[e], 1)
+                send_to(e, landing, sem)
+
+            @pl.when(plane + HOP == e)
+            def _():
+                remote(
+                    slot_out.at[pl.ds(plane + VIA[0], len(VIA))], relay, relay_sem.at[0], relay_sem.at[1], at_plane(e)
+                ).start()
+
+        for e in (*range(LOWER), *reversed(range(LAST, planes)), *range(LOWER, LAST)):
+            send(e)
+        for offset in VIA:
+
+            @pl.when(plane + offset < LAST)
+            def _():
+                pl.semaphore_wait(ready_sem.at[plane + offset], 1)
+
+        @pl.when(plane == 0)
         def _():
-            send_slots(slots[number].at[place * (high - low) + plane - low], recv_sem.at[number])
+            for k in range(1, side):
+                tell(go_sem.at[1], at_place(in_side(k)))
+            for other in range(LOWER, planes):
+                tell(go_sem.at[2], at_plane(other))
+
+        wait_for(relay_back, relay_sem.at[4])
+        for number in range(planes - LAST):
+            e = LAST + number
+            remote(
+                relay_back.at[number],
+                slots[1].at[place * (LOWER - EARLY) + plane],
+                relay_sem.at[5],
+                recv_sem.at[1],
+                at_plane(e),
+            ).start()
+
+        @pl.when(plane == 0)
+        def _():
+            pl.semaphore_wait(go_sem.at[1], side - 1)
+            for other in range(LAST, planes):
+                tell(go_sem.at[0], at_plane(other))
+
+    @pl.when(is_middle)
+    def _():
+        landing, sem = slots[1].at[place * (LOWER - EARLY) + plane - EARLY], recv_sem.at[1]
+        remote(
+            slot_out.at[pl.ds(LAST, planes - LAST)], relay_back, relay_sem.at[3], relay_sem.at[4], at_plane(plane - HOP)
+        ).start()
+        keep(landing, sem)
+
+        def send(e):
+            @pl.when(plane > e)
+            def _():
+                send_to(e, landing, sem)
+
+            @pl.when(plane < e)
+            def _():
+                pl.semaphore_wait(ready_sem.at[e], 1)
+                send_to(e, landing, sem)
+
+        def forward():
+            wait_for(relay, relay_sem.at[1])
+            for number, offset in enumerate(VIA):
+                e = plane + offset - HOP
+
+                @pl.when(e < LAST)
+                def _():
+                    remote(
+                        relay.at[number],
+                        slots[0].at[place * EARLY + plane - HOP],
+                        relay_sem.at[2],
+                        recv_sem.at[0],
+                        at_plane(e),
+                    ).start()
+
+        beyond = plane + VIA[-1] - HOP + 1
+        for e in range(LOWER):
+            send(e)
+        for e in range(LOWER, LAST):
+            pl.when(beyond == e)(forward)
+            send(e)
+
+        @pl.when(plane == LOWER - 1)
+        def _():
+            for k in range(1, side):
+                tell(go_sem.at[1], at_place(in_side(k)))
+            pl.semaphore_wait(go_sem.at[1], side - 1)
+            for other in range(LOWER, LAST):
+                tell(go_sem.at[0], at_plane(other))
+
+        pl.when(beyond >= LAST)(forward)
+
+    landing_high = slots[2].at[place * (planes - LOWER) + plane - LOWER]
+
+    @pl.when(is_high)
+    def _():
+        keep(landing_high, recv_sem.at[2])
+        for e in range(EARLY):
+            send_to(e, landing_high, recv_sem.at[2])
+
+    def send_next():
+        for e in range(EARLY, LOWER):
+            send_to(e, landing_high, recv_sem.at[2])
+
+    pl.when(jnp.logical_and(is_high, jnp.logical_not(is_last)))(send_next)
+
+    def send_high():
+        pl.semaphore_wait(go_sem.at[2], 1)
+        for e in range(LOWER, planes):
+
+            @pl.when(plane != e)
+            def _():
+                send_to(e, landing_high, recv_sem.at[2])
 
     top = jnp.max(logits, axis=0, keepdims=True)
     weight = jnp.exp(logits - top)
@@ -128,8 +293,9 @@
         low, high = chunks[number]
         rows = high - low
         wait_for(slots[number].at[pl.ds(0, (side - 1) * rows)], recv_sem.at[count + number])
+        block = slots[number][...]
         hidden = jnp.dot(
-            slots[number][...].reshape(side * rows, -1), w_in[...], preferred_element_type=F32
+            block.reshape(side * rows, -1), w_in[...], preferred_element_type=F32
         )
         hidden = jax.nn.gelu(hidden).astype(BF16)
         out = jnp.dot(hidden, w_out[...], preferred_element_type=F32)
@@ -165,8 +331,17 @@
                     own, expert_in.at[plane], send_sem.at[1 + 2 * count], recv_sem.at[3 * count], at_plane(target)
                 ).start()
 
+    @pl.when(is_high)
+    def _():
+        pl.semaphore_wait(go_sem.at[0], 1)
+
     spread(0)
+    @pl.when(is_high)
+    def _():
+        send_high()
+
     spread(1)
+    pl.when(is_last)(send_next)
     load_in.wait()
     load_out.wait()
     experts(0)
@@ -180,7 +355,36 @@
     wait_for(expert_in, recv_sem.at[3 * count])
     expert_ref[...] = expert_in[...].reshape(expert_ref.shape)
 
-    wait_for(slot_out.at[pl.ds(0, planes - 1)], send_sem.at[0])
+    @pl.when(is_early)
+    def _():
+        wait_for(relay, relay_sem.at[0])
+        wait_for(relay_back, relay_sem.at[5])
+
+    @pl.when(plane < EARLY - 1)
+    def _():
+        wait_for(slot_out.at[pl.ds(0, planes - 1 - len(VIA))], send_sem.at[0])
+
+    @pl.when(plane == EARLY - 1)
+    def _():
+        wait_for(slot_out.at[pl.ds(0, planes - len(VIA))], send_sem.at[0])
+
+    @pl.when(is_middle)
+    def _():
+        wait_for(slot_out.at[pl.ds(0, LAST - 1)], send_sem.at[0])
+        wait_for(relay_back, relay_sem.at[3])
+
+    @pl.when(jnp.logical_and(is_middle, plane < LOWER - 1))
+    def _():
+        wait_for(relay, relay_sem.at[2])
+
+    @pl.when(plane == LOWER - 1)
+    def _():
+        wait_for(relay.at[pl.ds(0, len(VIA) - 1)], relay_sem.at[2])
+
+    @pl.when(is_high)
+    def _():
+        wait_for(slot_out.at[pl.ds(0, planes - 1)], send_sem.at[0])
+
     for number, (low, high) in enumerate(chunks):
         others = pl.ds(0, (side - 1) * (high - low))
         wait_for(slots[number].at[others], send_sem.at[1 + number])
@@ -214,6 +418,8 @@
             pltpu.VMEM((width, units), BF16),
             pltpu.VMEM((units, width), BF16),
             rows(planes),
+            rows(len(VIA)),
+            rows(HOP),
             rows(devices),
             rows(devices),
             rows(devices),
@@ -222,6 +428,9 @@
             dma((3,)),
             dma((2 + 2 * len(CUTS),)),
             dma((1 + 3 * len(CUTS),)),
+            pltpu.SemaphoreType.REGULAR((planes,)),
+            pltpu.SemaphoreType.REGULAR((3,)),
+            dma((6,)),
         ],
         compiler_params=pltpu.CompilerParams(
             collective_id=0, has_side_effects=True, vmem_limit_bytes=60 * 1024 * 1024

time: 40.6 us -> 40.7 us (level)
  no operation moved by 1% of the time
where the time goes in v3:
time: 40.7 us; the launch traced here: 40.2 us
  Pallas kernels  39 us (96%)
  matrix products  1.2 us (3%)
    pallas_call x1, Pallas kernels, on_device(): pl.pallas_call(functools.partial(kernel, planes, side), out_shape=[pltpu....  39 us
    dot_general x1, matrix products, on_device(): lax.dot_general(combine, expert_out, (((0,), (0,)), ((), ())), preferred_...  1.2 us

profile of v3, /device:TPU:1, one launch (start us, length us, event | category | flops | bytes accessed | tf_op | source)
XLA Modules:
  0.0 40.2 jit_solution(8402151164164474788)
XLA Ops:
  0.0 39.0 %shard_map.46 = (bf16[16,256]{1,0:T(8,128)(2,1)S(1)}, bf16[16,1280]{1,0:T(8,128)(2,1)S(1)}) custom-call(bf16[1,256,1280]{2,1,0:T(8,128)(2,1)} %tokens_hbm.1, bf16[16,1280]{1,0:T(8,128)(2,1)} %bitcast.5, bf16[1280,640]{1,0:T(8,128)(2,1)} %w_in_hbm.1, bf16[640,1280]{1,0:T(8,128)(2,1)} %w_out_hbm.1), custom_call_target="tpu_custom_call" | custom-call | flops 419430400 | bytes 3276800 | tf_op jit(solution)/shard_map/pallas_call | solution.py:408
  39.0 1.2 %fusion = bf16[1,256,1280]{2,1,0:T(8,128)(2,1)} fusion(bf16[16,256]{1,0:T(8,128)(2,1)S(1)} %get-tuple-element.7, bf16[16,1280]{1,0:T(8,128)(2,1)S(1)} %get-tuple-element.8), kind=kOutput, calls=%fused_computation.1 | convolution fusion | flops 10813440 | bytes 704512 | tf_op jit(solution)/shard_map/dot_general | solution.py:442

commit v4 on v2

--- a/solution.py
+++ b/solution.py
@@ -10,7 +10,8 @@
 BF16 = jnp.bfloat16
 F32 = jnp.float32
 CORES = 2
-CUTS = (0, 4, 8)
+CUTS = (0, 2, 8)
+SIDE_ORDER = ((2, 0), (2, 1), (1, 0), (3, 0), (1, 1), (3, 1), (0, 1))
 
 
 def remote(src, dst, send_sem, recv_sem, target):
@@ -66,8 +67,13 @@
     def at_plane(other):
         return other * side + place
 
+    core = lax.rem(place, CORES)
+    columns = side // CORES
+
     def in_side(step):
-        return lax.rem(place + step, side)
+        column, other = SIDE_ORDER[step - 1]
+        column = lax.rem(lax.div(place, CORES) + column, columns)
+        return column * CORES + (1 - core if other else core)
 
     def at_place(other):
         return plane * side + other
@@ -167,10 +173,10 @@
 
     spread(0)
     spread(1)
+    spread(2)
     load_in.wait()
     load_out.wait()
     experts(0)
-    spread(2)
     experts(1)
     finish(0)
     experts(2)

time: 40.6 us -> 39.5 us (0.973)
  Pallas kernels: 39.2 us -> 38.2 us
    pallas_call x1, Pallas kernels: 39.2 us -> 38.2 us  [on_device(): pl.pallas_call(functools.partial(kernel, planes, side), out_shape=[pltpu....]
where the time goes in v4:
time: 39.5 us; the launch traced here: 39.4 us
  Pallas kernels  38.2 us (97%)
  matrix products  1.2 us (3%)
    pallas_call x1, Pallas kernels, on_device(): pl.pallas_call(functools.partial(kernel, planes, side), out_shape=[pltpu....  38.2 us
    dot_general x1, matrix products, on_device(): lax.dot_general(combine, expert_out, (((0,), (0,)), ((), ())), preferred_...  1.2 us

profile of v4, /device:TPU:1, one launch (start us, length us, event | category | flops | bytes accessed | tf_op | source)
XLA Modules:
  0.0 39.4 jit_solution(1314682030370012285)
XLA Ops:
  0.0 38.2 %shard_map.46 = (bf16[16,256]{1,0:T(8,128)(2,1)S(1)}, bf16[16,1280]{1,0:T(8,128)(2,1)S(1)}) custom-call(bf16[1,256,1280]{2,1,0:T(8,128)(2,1)} %tokens_hbm.1, bf16[16,1280]{1,0:T(8,128)(2,1)} %bitcast.5, bf16[1280,640]{1,0:T(8,128)(2,1)} %w_in_hbm.1, bf16[640,1280]{1,0:T(8,128)(2,1)} %w_out_hbm.1), custom_call_target="tpu_custom_call" | custom-call | flops 419430400 | bytes 3276800 | tf_op jit(solution)/shard_map/pallas_call | solution.py:210
  38.2 1.2 %fusion = bf16[1,256,1280]{2,1,0:T(8,128)(2,1)} fusion(bf16[16,256]{1,0:T(8,128)(2,1)S(1)} %get-tuple-element.7, bf16[16,1280]{1,0:T(8,128)(2,1)S(1)} %get-tuple-element.8), kind=kOutput, calls=%fused_computation.1 | convolution fusion | flops 10813440 | bytes 704512 | tf_op jit(solution)/shard_map/dot_general | solution.py:239

commit v5 on v4

--- a/solution.py
+++ b/solution.py
@@ -10,7 +10,7 @@
 BF16 = jnp.bfloat16
 F32 = jnp.float32
 CORES = 2
-CUTS = (0, 2, 8)
+CUTS = (0, 2, 4)
 SIDE_ORDER = ((2, 0), (2, 1), (1, 0), (3, 0), (1, 1), (3, 1), (0, 1))
 
 
@@ -45,6 +45,7 @@
     slots,
     partial,
     scattered,
+    direct,
     expert_out,
     expert_in,
     load_sem,
@@ -119,7 +120,21 @@
 
     top = jnp.max(logits, axis=0, keepdims=True)
     weight = jnp.exp(logits - top)
-    combine_ref[...] = (weight / jnp.sum(weight, axis=0, keepdims=True)).astype(BF16)
+    combine = (weight / jnp.sum(weight, axis=0, keepdims=True)).astype(BF16)
+    is_first = plane < CUTS[1]
+
+    @pl.when(is_first)
+    def _():
+        combine_ref[...] = jnp.broadcast_to(
+            combine[:, None, :], (planes, side, combine.shape[1])
+        ).reshape(combine_ref.shape)
+
+    @pl.when(jnp.logical_not(is_first))
+    def _():
+        combine_ref[:planes] = combine
+        combine_ref[planes:] = jnp.zeros((planes * (side - 1), combine.shape[1]), BF16)
+        expert_ref[planes:] = jnp.zeros((planes * (side - 1), expert_ref.shape[1]), BF16)
+
 
     def spread(number):
         low, high = chunks[number]
@@ -129,6 +144,23 @@
             remote(
                 block, block, send_sem.at[1 + number], recv_sem.at[count + number], at_place(in_side(k))
             ).start()
+
+    def send_direct():
+        here, sem = direct.at[me], recv_sem.at[2 * count]
+        for target in range(CUTS[1]):
+            for k in range(1, side):
+                to = in_side(k)
+                own = partial[0].at[to * CUTS[1] + target]
+                remote(own, here, send_sem.at[1 + count], sem, target * side + to).start()
+            own = partial[0].at[place * CUTS[1] + target]
+
+            @pl.when(plane == target)
+            def _():
+                pltpu.make_async_copy(own, here, sem).start()
+
+            @pl.when(plane != target)
+            def _():
+                remote(own, here, send_sem.at[1 + count], sem, target * side + place).start()
 
     def experts(number):
         low, high = chunks[number]
@@ -140,6 +172,8 @@
         hidden = jax.nn.gelu(hidden).astype(BF16)
         out = jnp.dot(hidden, w_out[...], preferred_element_type=F32)
         partial[number][...] = out.reshape(partial[number].shape).astype(BF16)
+        if number == 0:
+            return send_direct()
         block = scattered[number].at[pl.ds(place * rows, rows)]
         sem = recv_sem.at[2 * count + number]
         for k in range(1, side):
@@ -178,20 +212,36 @@
     load_out.wait()
     experts(0)
     experts(1)
-    finish(0)
     experts(2)
     finish(1)
     finish(2)
 
-    wait_for(expert_in, recv_sem.at[3 * count])
-    expert_ref[...] = expert_in[...].reshape(expert_ref.shape)
+    @pl.when(is_first)
+    def _():
+        wait_for(direct, recv_sem.at[2 * count])
+        expert_ref[...] = direct[...].reshape(expert_ref.shape)
+
+    @pl.when(jnp.logical_not(is_first))
+    def _():
+        wait_for(expert_in, recv_sem.at[3 * count])
+        expert_ref[:planes] = expert_in[...].reshape(planes, -1)
 
     wait_for(slot_out.at[pl.ds(0, planes - 1)], send_sem.at[0])
     for number, (low, high) in enumerate(chunks):
         others = pl.ds(0, (side - 1) * (high - low))
         wait_for(slots[number].at[others], send_sem.at[1 + number])
-        wait_for(partial[number].at[others], send_sem.at[1 + count + number])
-    wait_for(expert_out.at[pl.ds(0, planes - 1)], send_sem.at[1 + 2 * count])
+        if number > 0:
+            wait_for(partial[number].at[others], send_sem.at[1 + count + number])
+
+    @pl.when(is_first)
+    def _():
+        wait_for(partial[0].at[pl.ds(0, side * CUTS[1] - 1)], send_sem.at[1 + count])
+        wait_for(expert_out.at[pl.ds(0, planes - CUTS[1])], send_sem.at[1 + 2 * count])
+
+    @pl.when(jnp.logical_not(is_first))
+    def _():
+        wait_for(partial[0], send_sem.at[1 + count])
+        wait_for(expert_out.at[pl.ds(0, planes - CUTS[1] - 1)], send_sem.at[1 + 2 * count])
 
 
 def on_device(tokens, slot_weight, w_in, w_out, *, devices):
@@ -210,8 +260,8 @@
     combine, expert_out = pl.pallas_call(
         functools.partial(kernel, planes, side),
         out_shape=[
-            pltpu.VMEM((experts, patches), BF16),
-            pltpu.VMEM((experts, width), BF16),
+            pltpu.VMEM((devices, patches), BF16),
+            pltpu.VMEM((devices, width), BF16),
         ],
         in_specs=[hbm, vmem, hbm, hbm],
         out_specs=[vmem, vmem],
@@ -220,6 +270,7 @@
             pltpu.VMEM((width, units), BF16),
             pltpu.VMEM((units, width), BF16),
             rows(planes),
+            rows(devices),
             rows(devices),
             rows(devices),
             rows(devices),

time: 39.5 us -> 38.3 us (0.970)
  Pallas kernels: 38.2 us -> 36.9 us
    pallas_call x1, Pallas kernels: 38.2 us -> 36.9 us  [on_device(): pl.pallas_call(functools.partial(kernel, planes, side), out_shape=[pltpu....]
where the time goes in v5:
time: 38.3 us; the launch traced here: 38.1 us
  Pallas kernels  36.9 us (96%)
  matrix products  1.19 us (3%)
    pallas_call x1, Pallas kernels, on_device(): pl.pallas_call(functools.partial(kernel, planes, side), out_shape=[pltpu....  36.9 us
    dot_general x1, matrix products, on_device(): lax.dot_general(combine, expert_out, (((0,), (0,)), ((), ())), preferred_...  1.19 us

profile of v5, /device:TPU:1, one launch (start us, length us, event | category | flops | bytes accessed | tf_op | source)
XLA Modules:
  0.0 38.1 jit_solution(13690755886111808219)
XLA Ops:
  0.0 36.9 %shard_map.46 = (bf16[128,256]{1,0:T(8,128)(2,1)S(1)}, bf16[128,1280]{1,0:T(8,128)(2,1)S(1)}) custom-call(bf16[1,256,1280]{2,1,0:T(8,128)(2,1)} %tokens_hbm.1, bf16[16,1280]{1,0:T(8,128)(2,1)} %bitcast.5, bf16[1280,640]{1,0:T(8,128)(2,1)} %w_in_hbm.1, bf16[640,1280]{1,0:T(8,128)(2,1)} %w_out_hbm.1), custom_call_target="tpu_custom_call" | custom-call | flops 419430400 | bytes 3276800 | tf_op jit(solution)/shard_map/pallas_call | solution.py:260
  37.0 1.2 %fusion = bf16[1,256,1280]{2,1,0:T(8,128)(2,1)} fusion(bf16[128,256]{1,0:T(8,128)(2,1)S(1)} %get-tuple-element.7, bf16[128,1280]{1,0:T(8,128)(2,1)S(1)} %get-tuple-element.8), kind=kOutput, calls=%fused_computation.1 | convolution fusion | flops 84213760 | bytes 1048576 | tf_op jit(solution)/shard_map/dot_general | solution.py:290

commit v6 on v5

--- a/solution.py
+++ b/solution.py
@@ -33,11 +33,12 @@
     planes,
     side,
     tokens_hbm,
-    slot_ref,
+    slot_hbm,
     w_in_hbm,
     w_out_hbm,
     combine_ref,
     expert_ref,
+    slot_weight,
     tokens,
     w_in,
     w_out,
@@ -80,9 +81,9 @@
         return plane * side + other
 
     load_tokens = pltpu.make_async_copy(tokens_hbm, tokens, load_sem.at[0])
+    load_slot = pltpu.make_async_copy(slot_hbm, slot_weight, load_sem.at[3])
     load_in = pltpu.make_async_copy(w_in_hbm, w_in, load_sem.at[1])
     load_out = pltpu.make_async_copy(w_out_hbm, w_out, load_sem.at[2])
-    load_tokens.start()
     barrier = pltpu.get_barrier_semaphore()
     far_first = sorted(range(1, planes), key=lambda k: -min(k, planes - k))
     peers = [at_plane(in_plane(k)) for k in far_first]
@@ -91,12 +92,15 @@
         pl.semaphore_signal(
             barrier, inc=1, device_id={"expert": peer}, device_id_type=pl.DeviceIdType.MESH
         )
+    load_slot.start()
+    load_tokens.start()
     load_in.start()
     load_out.start()
 
+    load_slot.wait()
     load_tokens.wait()
     logits = lax.dot_general(
-        slot_ref[...], tokens[0], (((1,), (1,)), ((), ())), preferred_element_type=F32
+        slot_weight[...], tokens[0], (((1,), (1,)), ((), ())), preferred_element_type=F32
     )
     top = jnp.max(logits, axis=1, keepdims=True)
     weight = jnp.exp(logits - top)
@@ -125,14 +129,17 @@
 
     @pl.when(is_first)
     def _():
-        combine_ref[...] = jnp.broadcast_to(
-            combine[:, None, :], (planes, side, combine.shape[1])
-        ).reshape(combine_ref.shape)
+        combine_ref[...] = (
+            jnp.broadcast_to(combine[:, None, :], (planes, side, combine.shape[1]))
+            .reshape(planes * side, combine.shape[1])
+            .T
+        )
 
     @pl.when(jnp.logical_not(is_first))
     def _():
-        combine_ref[:planes] = combine
-        combine_ref[planes:] = jnp.zeros((planes * (side - 1), combine.shape[1]), BF16)
+        combine_ref[...] = jnp.concatenate(
+            [combine, jnp.zeros((planes * (side - 1), combine.shape[1]), BF16)]
+        ).T
         expert_ref[planes:] = jnp.zeros((planes * (side - 1), expert_ref.shape[1]), BF16)
 
 
@@ -260,12 +267,13 @@
     combine, expert_out = pl.pallas_call(
         functools.partial(kernel, planes, side),
         out_shape=[
-            pltpu.VMEM((devices, patches), BF16),
+            pltpu.VMEM((patches, devices), BF16),
             pltpu.VMEM((devices, width), BF16),
         ],
-        in_specs=[hbm, vmem, hbm, hbm],
+        in_specs=[hbm, hbm, hbm, hbm],
         out_specs=[vmem, vmem],
         scratch_shapes=[
+            pltpu.VMEM((experts, width), BF16),
             pltpu.VMEM(tokens.shape, BF16),
             pltpu.VMEM((width, units), BF16),
             pltpu.VMEM((units, width), BF16),
@@ -276,7 +284,7 @@
             rows(devices),
             rows(planes),
             rows(planes),
-            dma((3,)),
+            dma((4,)),
             dma((2 + 2 * len(CUTS),)),
             dma((1 + 3 * len(CUTS),)),
         ],
@@ -287,9 +295,7 @@
             flops=2 * 2 * devices * width * units, bytes_accessed=4 * width * units, transcendentals=0
         ),
     )(tokens, slot_weight.T, w_in, w_out)
-    mixed = lax.dot_general(
-        combine, expert_out, (((0,), (0,)), ((), ())), preferred_element_type=F32
-    )
+    mixed = jnp.dot(combine, expert_out, preferred_element_type=F32)
     return mixed.astype(BF16).reshape(tokens.shape)
 
 

time: 38.3 us -> 37.6 us (0.982)
  Pallas kernels: 36.9 us -> 36.3 us
    pallas_call x1, Pallas kernels: 36.9 us -> 36.3 us  [on_device(): pl.pallas_call(functools.partial(kernel, planes, side), out_shape=[pltpu....]
where the time goes in v6:
time: 37.6 us; the launch traced here: 37.4 us
  Pallas kernels  36.3 us (97%)
  matrix products  1.16 us (3%)
    pallas_call x1, Pallas kernels, on_device(): pl.pallas_call(functools.partial(kernel, planes, side), out_shape=[pltpu....  36.3 us
    dot_general x1, matrix products, on_device(): mixed = jnp.dot(combine, expert_out, preferred_element_type=F32)  1.16 us

profile of v6, /device:TPU:1, one launch (start us, length us, event | category | flops | bytes accessed | tf_op | source)
XLA Modules:
  0.0 37.4 jit_solution(16559756103502581987)
XLA Ops:
  0.0 36.3 %shard_map.46 = (bf16[256,128]{1,0:T(8,128)(2,1)S(1)}, bf16[128,1280]{1,0:T(8,128)(2,1)S(1)}) custom-call(bf16[1,256,1280]{2,1,0:T(8,128)(2,1)} %tokens_hbm.1, bf16[16,1280]{1,0:T(8,128)(2,1)} %bitcast.5, bf16[1280,640]{1,0:T(8,128)(2,1)} %w_in_hbm.1, bf16[640,1280]{1,0:T(8,128)(2,1)} %w_out_hbm.1), custom_call_target="tpu_custom_call" | custom-call | flops 419430400 | bytes 3276800 | tf_op jit(solution)/shard_map/pallas_call | solution.py:267
  36.3 1.2 %fusion = bf16[1,256,1280]{2,1,0:T(8,128)(2,1)} fusion(bf16[256,128]{1,0:T(8,128)(2,1)S(1)} %get-tuple-element.7, bf16[128,1280]{1,0:T(8,128)(2,1)S(1)} %get-tuple-element.8), kind=kOutput, calls=%fused_computation.1 | convolution fusion | flops 84213760 | bytes 1048576 | tf_op jit(solution)/shard_map/dot_general | solution.py:298

commit v7 on v6

--- a/solution.py
+++ b/solution.py
@@ -11,6 +11,8 @@
 F32 = jnp.float32
 CORES = 2
 CUTS = (0, 2, 4)
+PLACE_ORDER = (1, 0, 3, 2, 7, 6, 5, 4)
+MIX_PARTS = 4
 SIDE_ORDER = ((2, 0), (2, 1), (1, 0), (3, 0), (1, 1), (3, 1), (0, 1))
 
 
@@ -155,19 +157,17 @@
     def send_direct():
         here, sem = direct.at[me], recv_sem.at[2 * count]
         for target in range(CUTS[1]):
-            for k in range(1, side):
-                to = in_side(k)
+            for to in PLACE_ORDER:
                 own = partial[0].at[to * CUTS[1] + target]
-                remote(own, here, send_sem.at[1 + count], sem, target * side + to).start()
-            own = partial[0].at[place * CUTS[1] + target]
-
-            @pl.when(plane == target)
-            def _():
-                pltpu.make_async_copy(own, here, sem).start()
-
-            @pl.when(plane != target)
-            def _():
-                remote(own, here, send_sem.at[1 + count], sem, target * side + place).start()
+                is_own = me == target * side + to
+
+                @pl.when(is_own)
+                def _():
+                    pltpu.make_async_copy(own, here, sem).start()
+
+                @pl.when(jnp.logical_not(is_own))
+                def _():
+                    remote(own, here, send_sem.at[1 + count], sem, target * side + to).start()
 
     def experts(number):
         low, high = chunks[number]
@@ -295,8 +295,30 @@
             flops=2 * 2 * devices * width * units, bytes_accessed=4 * width * units, transcendentals=0
         ),
     )(tokens, slot_weight.T, w_in, w_out)
-    mixed = jnp.dot(combine, expert_out, preferred_element_type=F32)
-    return mixed.astype(BF16).reshape(tokens.shape)
+    part_rows = patches // MIX_PARTS
+
+    def mix(combine_ref, expert_ref, out_hbm, out, sem):
+        parts = [pl.ds(part * part_rows, part_rows) for part in range(MIX_PARTS)]
+        copies = [
+            pltpu.make_async_copy(out.at[part], out_hbm.at[0, part], sem.at[number])
+            for number, part in enumerate(parts)
+        ]
+        for part, copy in zip(parts, copies):
+            out[part] = jnp.dot(
+                combine_ref[part], expert_ref[...], preferred_element_type=F32
+            ).astype(BF16)
+            copy.start()
+        for copy in copies:
+            copy.wait()
+
+    return pl.pallas_call(
+        mix,
+        out_shape=jax.ShapeDtypeStruct(tokens.shape, BF16),
+        in_specs=[vmem, vmem],
+        out_specs=hbm,
+        scratch_shapes=[pltpu.VMEM((patches, width), BF16), dma((MIX_PARTS,))],
+        compiler_params=pltpu.CompilerParams(vmem_limit_bytes=8 * 1024 * 1024),
+    )(combine, expert_out)
 
 
 def solution(mesh):

time: 37.6 us -> 37.3 us (level)
  matrix products: 1.16 us -> 0 us
  Pallas kernels: 36.3 us -> 37.2 us
    dot_general x1 -> x0, matrix products: 1.16 us -> none  [on_device(): mixed = jnp.dot(combine, expert_out, preferred_element_type=F32)]
    pallas_call x0 -> x1, Pallas kernels: none -> 1.07 us  [on_device(): pl.pallas_call(mix, out_shape=jax.ShapeDtypeStruct(tokens.shape, BF16), i...]
where the time goes in v7:
time: 37.3 us; the launch traced here: 37.2 us
  Pallas kernels  37.2 us (100%)
    pallas_call x1, Pallas kernels, on_device(): pl.pallas_call(functools.partial(kernel, planes, side), out_shape=[pltpu....  36.1 us
    pallas_call x1, Pallas kernels, on_device(): pl.pallas_call(mix, out_shape=jax.ShapeDtypeStruct(tokens.shape, BF16), i...  1.07 us

profile of v7, /device:TPU:1, one launch (start us, length us, event | category | flops | bytes accessed | tf_op | source)
XLA Modules:
  0.0 37.2 jit_solution(4157649859164883693)
XLA Ops:
  0.0 36.1 %shard_map.46 = (bf16[256,128]{1,0:T(8,128)(2,1)S(1)}, bf16[128,1280]{1,0:T(8,128)(2,1)S(1)}) custom-call(bf16[1,256,1280]{2,1,0:T(8,128)(2,1)} %tokens_hbm.1, bf16[16,1280]{1,0:T(8,128)(2,1)} %bitcast.1, bf16[1280,640]{1,0:T(8,128)(2,1)} %w_in_hbm.1, bf16[640,1280]{1,0:T(8,128)(2,1)} %w_out_hbm.1), custom_call_target="tpu_custom_call" | custom-call | flops 419430400 | bytes 3276800 | tf_op jit(solution)/shard_map/pallas_call | solution.py:267
  36.1 1.1 %shard_map.47 = bf16[1,256,1280]{2,1,0:T(8,128)(2,1)} custom-call(bf16[256,128]{1,0:T(8,128)(2,1)S(1)} %get-tuple-element.7.combine_ref, bf16[128,1280]{1,0:T(8,128)(2,1)S(1)} %get-tuple-element.8.expert_ref), custom_call_target="tpu_custom_call" | custom-call | tf_op jit(solution)/shard_map/pallas_call | solution.py:314

commit v8 on v7

--- a/solution.py
+++ b/solution.py
@@ -10,6 +10,7 @@
 BF16 = jnp.bfloat16
 F32 = jnp.float32
 CORES = 2
+LATE = (6, 12)
 CUTS = (0, 2, 4)
 PLACE_ORDER = (1, 0, 3, 2, 7, 6, 5, 4)
 MIX_PARTS = 4
@@ -155,7 +156,8 @@
             ).start()
 
     def send_direct():
-        here, sem = direct.at[me], recv_sem.at[2 * count]
+        is_late = jnp.logical_and(plane >= LATE[0], plane < LATE[1])
+        here, sem = direct.at[me], recv_sem.at[jnp.where(is_late, 2 * count, 3 * count + 1)]
         for target in range(CUTS[1]):
             for to in PLACE_ORDER:
                 own = partial[0].at[to * CUTS[1] + target]
@@ -223,16 +225,6 @@
     finish(1)
     finish(2)
 
-    @pl.when(is_first)
-    def _():
-        wait_for(direct, recv_sem.at[2 * count])
-        expert_ref[...] = direct[...].reshape(expert_ref.shape)
-
-    @pl.when(jnp.logical_not(is_first))
-    def _():
-        wait_for(expert_in, recv_sem.at[3 * count])
-        expert_ref[:planes] = expert_in[...].reshape(planes, -1)
-
     wait_for(slot_out.at[pl.ds(0, planes - 1)], send_sem.at[0])
     for number, (low, high) in enumerate(chunks):
         others = pl.ds(0, (side - 1) * (high - low))
@@ -249,6 +241,22 @@
     def _():
         wait_for(partial[0], send_sem.at[1 + count])
         wait_for(expert_out.at[pl.ds(0, planes - CUTS[1] - 1)], send_sem.at[1 + 2 * count])
+
+    @pl.when(is_first)
+    def _():
+        soon = planes - LATE[1] + LATE[0]
+        wait_for(direct.at[pl.ds(0, soon * side)], recv_sem.at[3 * count + 1])
+        for low, high in ((0, LATE[0]), (LATE[1], planes)):
+            part = slice(low * side, high * side)
+            expert_ref[part] = direct[part].reshape((high - low) * side, -1)
+        part = slice(LATE[0] * side, LATE[1] * side)
+        wait_for(direct.at[pl.ds(part.start, part.stop - part.start)], recv_sem.at[2 * count])
+        expert_ref[part] = direct[part].reshape(part.stop - part.start, -1)
+
+    @pl.when(jnp.logical_not(is_first))
+    def _():
+        wait_for(expert_in, recv_sem.at[3 * count])
+        expert_ref[:planes] = expert_in[...].reshape(planes, -1)
 
 
 def on_device(tokens, slot_weight, w_in, w_out, *, devices):
@@ -286,7 +294,7 @@
             rows(planes),
             dma((4,)),
             dma((2 + 2 * len(CUTS),)),
-            dma((1 + 3 * len(CUTS),)),
+            dma((2 + 3 * len(CUTS),)),
         ],
         compiler_params=pltpu.CompilerParams(
             collective_id=0, has_side_effects=True, vmem_limit_bytes=60 * 1024 * 1024

time: 37.3 us -> 37.2 us (level)
  no operation moved by 1% of the time
where the time goes in v8:
time: 37.2 us; the launch traced here: 37.1 us
  Pallas kernels  37.1 us (100%)
    pallas_call x1, Pallas kernels, on_device(): pl.pallas_call(functools.partial(kernel, planes, side), out_shape=[pltpu....  36 us
    pallas_call x1, Pallas kernels, on_device(): pl.pallas_call(mix, out_shape=jax.ShapeDtypeStruct(tokens.shape, BF16), i...  1.07 us

profile of v8, /device:TPU:1, one launch (start us, length us, event | category | flops | bytes accessed | tf_op | source)
XLA Modules:
  0.0 37.1 jit_solution(8420501055683761075)
XLA Ops:
  0.0 36.0 %shard_map.46 = (bf16[256,128]{1,0:T(8,128)(2,1)S(1)}, bf16[128,1280]{1,0:T(8,128)(2,1)S(1)}) custom-call(bf16[1,256,1280]{2,1,0:T(8,128)(2,1)} %tokens_hbm.1, bf16[16,1280]{1,0:T(8,128)(2,1)} %bitcast.1, bf16[1280,640]{1,0:T(8,128)(2,1)} %w_in_hbm.1, bf16[640,1280]{1,0:T(8,128)(2,1)} %w_out_hbm.1), custom_call_target="tpu_custom_call" | custom-call | flops 419430400 | bytes 3276800 | tf_op jit(solution)/shard_map/pallas_call | solution.py:275
  36.1 1.1 %shard_map.47 = bf16[1,256,1280]{2,1,0:T(8,128)(2,1)} custom-call(bf16[256,128]{1,0:T(8,128)(2,1)S(1)} %get-tuple-element.7.combine_ref, bf16[128,1280]{1,0:T(8,128)(2,1)S(1)} %get-tuple-element.8.expert_ref), custom_call_target="tpu_custom_call" | custom-call | tf_op jit(solution)/shard_map/pallas_call | solution.py:322

commit v9 on v7

--- a/solution.py
+++ b/solution.py
@@ -13,7 +13,7 @@
 CUTS = (0, 2, 4)
 PLACE_ORDER = (1, 0, 3, 2, 7, 6, 5, 4)
 MIX_PARTS = 4
-SIDE_ORDER = ((2, 0), (2, 1), (1, 0), (3, 0), (1, 1), (3, 1), (0, 1))
+SIDE_ORDER = ((2, 0), (2, 1), (3, 0), (1, 0), (3, 1), (1, 1), (0, 1))
 
 
 def remote(src, dst, send_sem, recv_sem, target):

time: 37.3 us -> 37.3 us (level)
  no operation moved by 1% of the time
where the time goes in v9:
time: 37.3 us; the launch traced here: 37.2 us
  Pallas kernels  37.2 us (100%)
    pallas_call x1, Pallas kernels, on_device(): pl.pallas_call(functools.partial(kernel, planes, side), out_shape=[pltpu....  36.1 us
    pallas_call x1, Pallas kernels, on_device(): pl.pallas_call(mix, out_shape=jax.ShapeDtypeStruct(tokens.shape, BF16), i...  1.07 us

profile of v9, /device:TPU:1, one launch (start us, length us, event | category | flops | bytes accessed | tf_op | source)
XLA Modules:
  0.0 37.2 jit_solution(6294516652698403811)
XLA Ops:
  0.0 36.1 %shard_map.46 = (bf16[256,128]{1,0:T(8,128)(2,1)S(1)}, bf16[128,1280]{1,0:T(8,128)(2,1)S(1)}) custom-call(bf16[1,256,1280]{2,1,0:T(8,128)(2,1)} %tokens_hbm.1, bf16[16,1280]{1,0:T(8,128)(2,1)} %bitcast.1, bf16[1280,640]{1,0:T(8,128)(2,1)} %w_in_hbm.1, bf16[640,1280]{1,0:T(8,128)(2,1)} %w_out_hbm.1), custom_call_target="tpu_custom_call" | custom-call | flops 419430400 | bytes 3276800 | tf_op jit(solution)/shard_map/pallas_call | solution.py:267
  36.1 1.1 %shard_map.47 = bf16[1,256,1280]{2,1,0:T(8,128)(2,1)} custom-call(bf16[256,128]{1,0:T(8,128)(2,1)S(1)} %get-tuple-element.7.combine_ref, bf16[128,1280]{1,0:T(8,128)(2,1)S(1)} %get-tuple-element.8.expert_ref), custom_call_target="tpu_custom_call" | custom-call | tf_op jit(solution)/shard_map/pallas_call | solution.py:314
